TPU v7x, 32 devices: a whole 2x2x4 slice. The times are simulated.
32 devices in a mesh: groups: 2 (over y), ctx: 4 (over z), head: 2 (over x), sub: 2 (over core).
Axes of the slice: x: 2, y: 2, z: 4, core: 2. Of those that a mesh axis runs over, the one named last changes fastest.
Arguments:
- queries: bfloat16 [4096, 40, 128], P(('groups', 'ctx', 'sub'), 'head'), parts along dimension 0, may hold values from -35 to 35
- key_rows: bfloat16 [4096, 40, 128], P(('groups', 'ctx', 'sub'), 'head'), parts along dimension 0, may hold values from -4.5 to 4.5
- value_rows: bfloat16 [4096, 40, 128], P(('groups', 'ctx', 'sub'), 'head'), parts along dimension 0, may hold values from -16 to 16
- critical: int32 [64, 40, 16], P(('groups', 'ctx', 'sub'), 'head'), parts along dimension 0, may hold values from 0 to 31, as said below
- branch_weight: bfloat16 [128, 128], replicated, may hold values from -0.5 to 0.5
Outputs:
- attended: bfloat16 [4096, 40, 128], P(('groups', 'ctx', 'sub'), 'head'), parts along dimension 0
There are 2 independent parts, one for each index of `groups`. A program takes and returns all parts, laid end to end along the dimension named above; an argument that names none is the same for every part. Nothing has to cross between parts.
Inputs may be any that keep to these rules, and one draw needn't show every extreme that they name: Each list critical[b, h, :] names 16 different key blocks. Its first entry is b itself, the next 3 are the following blocks of b's segment of 256 consecutive tokens, cyclically within the segment; the other 12 lie in other segments. Over all lists of one segment's query blocks and one group of 20 consecutive heads, at most 58 different (block, head) pairs lie in any one other segment, and exactly 58 in some.
All inputs are finite; a program needn't handle non-finite values.
Results may differ from a plain program's by a relative error of at most 0.004.
Values may be sent and summed in bfloat16 or wider, within the bound.
A program may use at most 128 MiB of HBM per device.

v0:
```python
import jax
import jax.numpy as jnp
from jax import lax
from jax.sharding import PartitionSpec as P


def as_sent(array):

    def short(part):
        return part.astype(jnp.bfloat16) if part.dtype == jnp.float32 else part

    return jax.tree.map(short, array)


def feature(values_in):
    return jax.nn.elu(values_in) + 1.0


def attend_pair(inputs, pool_keys, pool_values, branch_weight, softmax_scale):
    query_block_rows, query_feature, pool_index, pair_state, pair_total = inputs
    block_count = query_block_rows.shape[0]
    head_width = query_block_rows.shape[-1]
    nearby_key_rows = jnp.take(pool_keys, pool_index.reshape(-1), axis=0).reshape(
        block_count, 2, -1, head_width
    )
    nearby_value_rows = jnp.take(pool_values, pool_index.reshape(-1), axis=0).reshape(
        block_count, 2, -1, head_width
    )
    score_matrix = (
        jnp.einsum(
            "bhqd,bhkd->bhqk", query_block_rows, nearby_key_rows, preferred_element_type=jnp.float32
        )
        * softmax_scale
    )
    top_score = jnp.max(score_matrix, axis=-1, keepdims=True)
    expo_scores = jnp.exp(score_matrix - top_score)
    softmax_weights = (expo_scores / jnp.sum(expo_scores, axis=-1, keepdims=True)).astype(
        jnp.bfloat16
    )
    sparse_output = jnp.einsum(
        "bhqk,bhkd->bhqd", softmax_weights, nearby_value_rows, preferred_element_type=jnp.float32
    )
    nearby_key_features = feature(nearby_key_rows.astype(jnp.float32)).astype(jnp.bfloat16)
    nearby_score_matrix = jnp.einsum(
        "bhqd,bhkd->bhqk", query_feature, nearby_key_features, preferred_element_type=jnp.float32
    )
    nearby_weight_matrix = nearby_score_matrix.astype(jnp.bfloat16)
    nearby_numerator = jnp.einsum(
        "bhqk,bhkd->bhqd",
        nearby_weight_matrix,
        nearby_value_rows,
        preferred_element_type=jnp.float32,
    )
    nearby_denominator = jnp.sum(nearby_score_matrix, axis=-1)
    feature_wide = query_feature.astype(jnp.float32)
    linear_numerator = (
        jnp.einsum("bhqd,hde->bhqe", feature_wide, pair_state, precision=lax.Precision.HIGHEST)
        - nearby_numerator
    )
    linear_denominator = (
        jnp.einsum("bhqd,hd->bhq", feature_wide, pair_total, precision=lax.Precision.HIGHEST)
        - nearby_denominator
    )
    linear_part = (linear_numerator / linear_denominator[..., None]).astype(jnp.bfloat16)
    projected = jnp.einsum(
        "bhqd,de->bhqe", linear_part, branch_weight, preferred_element_type=jnp.float32
    )
    return (sparse_output + projected).astype(jnp.bfloat16)


def on_device(queries, key_rows, value_rows, critical, branch_weight):
    row_count, head_count, head_width = queries.shape
    list_length = critical.shape[-1]
    block_count = row_count // 64
    shard_count = lax.axis_size(("ctx", "sub"))
    myself = lax.axis_index(("ctx", "sub"))
    local_count = min(block_count, 8)
    pool_size = 24 - local_count
    capacity = (head_count * pool_size + shard_count - 2) // (shard_count - 1)
    softmax_scale = head_width ** (-0.5)
    key_feature = feature(key_rows.astype(jnp.float32)).astype(jnp.bfloat16)
    query_feature = feature(queries.astype(jnp.float32)).astype(jnp.bfloat16)
    kv_state = jnp.einsum(
        "thd,the->hde", key_feature, value_rows, preferred_element_type=jnp.float32
    )
    key_total = jnp.sum(key_feature, axis=0, dtype=jnp.float32)
    kv_state, key_total = lax.psum((kv_state, key_total), ("ctx", "sub"))
    pair_slots = block_count * head_count
    block_owner = critical // block_count
    block_local = critical % block_count
    slot_code = block_local * head_count + jnp.arange(head_count, dtype=jnp.int32)[None, :, None]
    every_block = jnp.arange(shard_count * block_count, dtype=jnp.int32)
    hit_counts = jnp.sum((critical[..., None] == every_block).astype(jnp.int32), axis=(0, 2))
    wanted = (
        hit_counts.reshape(head_count, shard_count, block_count)
        .transpose(1, 2, 0)
        .reshape(shard_count, pair_slots)
        > 0
    )
    wanted = jnp.logical_and(wanted, jnp.arange(shard_count, dtype=jnp.int32)[:, None] != myself)
    slot_place = jnp.cumsum(wanted.astype(jnp.int32), axis=1) - 1
    slot_match = jnp.logical_and(
        wanted[:, :, None],
        slot_place[:, :, None] == jnp.arange(capacity, dtype=jnp.int32)[None, None, :],
    )
    code_values = jnp.sum(
        jnp.where(slot_match, jnp.arange(pair_slots, dtype=jnp.int32)[None, :, None], 0), axis=1
    )
    asked_codes = jnp.where(jnp.any(slot_match, axis=1), code_values, -1)
    local_keys = (
        key_rows.reshape(block_count, 64, head_count, head_width)
        .transpose(0, 2, 1, 3)
        .reshape(pair_slots, 64, head_width)
    )
    local_values = (
        value_rows.reshape(block_count, 64, head_count, head_width)
        .transpose(0, 2, 1, 3)
        .reshape(pair_slots, 64, head_width)
    )
    picked = jnp.clip(
        lax.all_to_all(asked_codes, ("ctx", "sub"), split_axis=0, concat_axis=0, tiled=True),
        0,
        pair_slots - 1,
    )
    far_keys, far_values = lax.all_to_all(
        as_sent((jnp.take(local_keys, picked, axis=0), jnp.take(local_values, picked, axis=0))),
        ("ctx", "sub"),
        split_axis=0,
        concat_axis=0,
        tiled=True,
    )
    pool_keys = jnp.concatenate(
        [local_keys, far_keys.reshape(shard_count * capacity, 64, head_width)], axis=0
    )
    pool_values = jnp.concatenate(
        [local_values, far_values.reshape(shard_count * capacity, 64, head_width)], axis=0
    )
    flat_index = block_owner * pair_slots + slot_code
    slot_table = jnp.where(wanted, slot_place, 0).reshape(-1)
    table_range = jnp.arange(shard_count * pair_slots, dtype=jnp.int32)
    slot_found = jnp.sum(jnp.where(flat_index[..., None] == table_range, slot_table, 0), axis=-1)
    pool_index = jnp.where(
        block_owner == myself, slot_code, pair_slots + block_owner * capacity + slot_found
    )
    pair_count = head_count // 2
    query_pairs = queries.reshape(block_count, 64, pair_count, 2, head_width).transpose(
        2, 0, 3, 1, 4
    )
    feature_pairs = query_feature.reshape(block_count, 64, pair_count, 2, head_width).transpose(
        2, 0, 3, 1, 4
    )
    index_pairs = pool_index.reshape(block_count, pair_count, 2, list_length).transpose(1, 0, 2, 3)
    state_pairs = kv_state.reshape(pair_count, 2, head_width, head_width)
    total_pairs = key_total.reshape(pair_count, 2, head_width)
    attended = lax.map(
        lambda inputs: attend_pair(inputs, pool_keys, pool_values, branch_weight, softmax_scale),
        (query_pairs, feature_pairs, index_pairs, state_pairs, total_pairs),
    )
    return attended.transpose(1, 3, 0, 2, 4).reshape(row_count, head_count, head_width)


def solution(mesh):
    in_specs = (
        P(("groups", "ctx", "sub"), "head", None),
        P(("groups", "ctx", "sub"), "head", None),
        P(("groups", "ctx", "sub"), "head", None),
        P(("groups", "ctx", "sub"), "head", None),
        P(),
    )
    out_specs = P(("groups", "ctx", "sub"), "head", None)
    return jax.shard_map(
        on_device, mesh=mesh, in_specs=in_specs, out_specs=out_specs, check_vma=False
    )
```

profile of v0, /device:TPU:0, one launch (start us, length us, event | category | flops | bytes accessed | tf_op | source)
XLA Modules:
  0.0 728.4 jit_solution(15897045216261678019)
XLA Ops:
  11.0 6.3 all-to-all-start
  22.9 13.3 %gather_fusion.2 = bf16[464,64,128]{2,1,0:T(8,128)(2,1)} fusion(bf16[80,64,128]{2,1,0:T(8,128)(2,1)S(1)} %bitcast.121, s32[1024]{0:T(1024)S(1)} %pad_clamp_fusion.1), kind=kCustom, calls=%fused_computation.clone | custom fusion | bytes 15206208 | tf_op jit(solution)/shard_map/jit(_take)/gather | solution.py:126
  36.3 13.3 %gather_fusion.3 = bf16[464,64,128]{2,1,0:T(8,128)(2,1)} fusion(bf16[80,64,128]{2,1,0:T(8,128)(2,1)S(1)} %bitcast.123, s32[1024]{0:T(1024)S(1)} %pad_clamp_fusion.1), kind=kCustom, calls=%fused_computation.2.clone | custom fusion | bytes 15206208 | tf_op jit(solution)/shard_map/jit(_take)/gather | solution.py:126
  49.6 8.8 %broadcast_select_fusion.2 = (bf16[8,58,64,128]{3,2,1,0:T(8,128)(2,1)S(1)}, bf16[8,58,64,128]{3,2,1,0:T(8,128)(2,1)}) fusion(bf16[8,58,64,128]{3,2,1,0:T(8,128)(2,1)} %bitcast.127, pred[8,58]{1,0:T(8,128)(4,1)S(1)} %compare_and_fusion.1, bf16[8,58,64,128]{3,2,1,0:T(8,128)(2,1)} %bitcast.126), kind=kLoop, calls=%fused_computation.57 | loop fusion | flops 7602176 | bytes 30409168 | tf_op jit(solution)/shard_map/jit(_take)/select_n | solution.py:126
  58.4 170.7 %all_to_all.16 = bf16[8,58,64,128]{3,2,1,0:T(8,128)(2,1)} all-to-all(bf16[8,58,64,128]{3,2,1,0:T(8,128)(2,1)S(1)} %get-tuple-element.128), channel_id=1, replica_groups=mesh['groups'=2,'ctx'=4,'head'=2,'sub'=2] {'ctx','sub'}, dimensions={0} | all-to-all | bytes 15204352 | tf_op jit(solution)/shard_map/all_to_all | solution.py:125
  243.2 197.0 %psum.15 = f32[10,2,128]{2,1,0:T(2,128)S(1)} all-reduce(f32[10,2,128]{2,1,0:T(2,128)S(1)} %reshape.134), channel_id=1, replica_groups=mesh['groups'=2,'ctx'=4,'head'=2,'sub'=2] {'ctx','sub'}, use_global_device_ids=true, to_apply=%region_5.6 | all-reduce | flops 2560 | bytes 20480 | tf_op jit(solution)/shard_map/psum | solution.py:87
  443.8 7.3 %pad_maximum_fusion.1 = bf16[544,64,128]{2,1,0:T(8,128)(2,1)} fusion(bf16[464,64,128]{2,1,0:T(8,128)(2,1)} %bitcast.125, bf16[80,64,128]{2,1,0:T(8,128)(2,1)S(1)} %bitcast.124), kind=kLoop, calls=%fused_computation.52 | loop fusion | flops 4456448 | bytes 17825792 | tf_op jit(solution)/shard_map/concatenate | solution.py:135
  451.2 7.4 %pad_maximum_fusion = bf16[544,64,128]{2,1,0:T(8,128)(2,1)} fusion(bf16[464,64,128]{2,1,0:T(8,128)(2,1)} %bitcast.29, bf16[80,64,128]{2,1,0:T(8,128)(2,1)S(1)} %bitcast.122), kind=kLoop, calls=%fused_computation.51 | loop fusion | flops 4456448 | bytes 17825792 | tf_op jit(solution)/shard_map/concatenate | solution.py:132
  458.6 260.5 %while.10 = (s32[]{:T(128)}, bf16[10,4,2,64,128]{4,3,2,1,0:T(8,128)(2,1)}, bf16[10,4,2,64,128]{4,3,1,2,0:T(8,128)(2,1)}, s32[10,4,2,16]{3,1,2,0:T(4,128)S(1)}, b...) while((s32[]{:T(128)}, ...), condition=%wide.region_12.15_spmd, body=%wide.region_8.14_spmd.sunk | while | flops 668537472 | bytes 44628372 | solution.py:155
  458.7 5.7 gather_fusion
  464.4 5.7 gather_fusion.1
  484.7 5.7 gather_fusion
  490.4 5.7 gather_fusion.1
  510.8 5.7 gather_fusion
  516.5 5.7 gather_fusion.1
  536.8 5.7 gather_fusion
  542.5 5.7 gather_fusion.1
  568.6 5.7 gather_fusion.1
  594.6 5.7 gather_fusion.1
  620.7 5.7 gather_fusion.1
  646.7 5.7 gather_fusion.1
  667.1 5.7 gather_fusion
  672.8 5.7 gather_fusion.1
  698.8 5.7 gather_fusion.1
  (250 shorter events, 204.3 us)
Async XLA Ops:
  11.0 11.8 %all-to-all-start = ((s32[8,1,58]{2,1,0:T(1,128)}), s32[8,1,58]{2,1,0:T(1,128)S(1)}, u32[]{:S(2)}, u32[]{:S(2)}) async-start(s32[8,1,58]{2,1,0:T(1,128)} %copy.55), calls=%async_computation | async-start | bytes 8192 | tf_op jit(solution)/shard_map/all_to_all | solution.py:121
  17.3 1.7 copy-start.1
  229.1 222.0 %all-to-all-start.1 = ((bf16[8,58,64,128]{3,2,1,0:T(8,128)(2,1)}), bf16[8,58,64,128]{3,2,1,0:T(8,128)(2,1)}, u32[]{:S(2)}, u32[]{:S(2)}) async-start(bf16[8,58,64,128]{3,2,1,0:T(8,128)(2,1)} %get-tuple-element.129), calls=%async_computation.1 | async-start | bytes 15204352 | tf_op jit(solution)/shard_map/all_to_all | solution.py:125
  234.2 224.3 %all-reduce.2.cloned.1.call-start = ((), (), s32[]{:S(2)}) async-start(), calls=%async_computation.3 | async-start | bytes 2621440 | tf_op jit(solution)/shard_map/psum | solution.py:87
  451.2 7.4 %copy-start.2 = (bf16[128,128]{1,0:T(8,128)(2,1)S(1)}, bf16[128,128]{1,0:T(8,128)(2,1)}, u32[]{:S(2)}) copy-start(bf16[128,128]{1,0:T(8,128)(2,1)} %param.15) | copy-start | bytes 98308
  479.0 1.4 copy-start
  505.1 1.4 copy-start
  531.1 1.4 copy-start
  557.2 1.4 copy-start
  583.2 1.4 copy-start
  609.3 1.4 copy-start
  635.3 1.4 copy-start
  661.4 1.4 copy-start
  687.4 1.4 copy-start
  713.4 1.4 copy-start
Sparse Core Ops, SparseCore 0:
  238.6 151.0 all-reduce.1
where the time goes:
time: 730 us; the launch traced here: 728 us
  blocking collectives  368 us (50%)
  local copies, waits for them, and re-layouts  172 us (24%)
  matrix products  91.4 us (13%)
  other arithmetic  68.2 us (9%)
  between operations  13.5 us (2%)
  starting transfers between devices  11.5 us (2%)
    psum x1, blocking collectives, on_device(): kv_state, key_total = lax.psum((kv_state, key_total), ('ctx', 'sub'))  197 us
    all_to_all x1, blocking collectives, on_device(): lax.all_to_all(as_sent((jnp.take(local_keys, picked, axis=0), jnp.take(lo...  171 us
    gather x10, local copies, waits for them, and re-layouts, attend_pair(): jnp.take(pool_values, pool_index.reshape(-1), axis=0)  57.2 us
    gather x10, local copies, waits for them, and re-layouts, attend_pair(): jnp.take(pool_keys, pool_index.reshape(-1), axis=0)  57 us
    dot_general x10, matrix products, attend_pair(): jnp.einsum('bhqk,bhkd->bhqd', softmax_weights, nearby_value_rows, preferr...  26.9 us
    select_n x20, other arithmetic, attend_pair(): jnp.take(pool_keys, pool_index.reshape(-1), axis=0)  26.7 us
    dot_general x10, matrix products, attend_pair(): jnp.einsum('bhqd,bhkd->bhqk', query_feature, nearby_key_features, preferr...  22.8 us
  transfers between devices with their start and end apart: 3, of which 1 were waited for; matrix products, arithmetic and copies ran while one was open for 4% of the time, Pallas kernels for 0%

commit v1 on v0

--- a/solution.py
+++ b/solution.py
@@ -1,6 +1,11 @@
+import functools
+import math
+
 import jax
 import jax.numpy as jnp
 from jax import lax
+from jax.experimental import pallas as pl
+from jax.experimental.pallas import tpu as pltpu
 from jax.sharding import PartitionSpec as P
 
 
@@ -159,6 +164,327 @@
     return attended.transpose(1, 3, 0, 2, 4).reshape(row_count, head_count, head_width)
 
 
+BLOCK = 64
+
+
+def wide_feature(rows):
+    wide = rows.astype(jnp.float32)
+    return jnp.where(wide > 0, wide + 1.0, jnp.exp(jnp.minimum(wide, 0.0)))
+
+
+def by_heads_kernel(dims, *refs):
+    chips, heads, rows, width, listed = dims
+    q_ref, k_ref, v_ref, lists_ref, weight_ref, out_ref = refs[:6]
+    refs = refs[6:]
+    q_bufs, refs = refs[:heads], refs[heads:]
+    k_bufs, refs = refs[:heads], refs[heads:]
+    v_bufs, refs = refs[:heads], refs[heads:]
+    o_bufs, refs = refs[:heads], refs[heads:]
+    (lists_in, lists, states, totals, state_sum, total_sum) = refs[:6]
+    (send, recv, own, pair_send, pair_recv, out_send, out_recv, out_own) = refs[6:14]
+    list_send, list_recv, list_own = refs[14:]
+    group = lax.axis_index("groups")
+    chip = lax.axis_index("ctx")
+    column = lax.axis_index("head")
+    core = lax.axis_index("sub")
+    blocks = rows // BLOCK
+    half = chips * blocks
+    mate = (group, chip, column, 1 - core)
+
+    def peer(step):
+        other = lax.rem(chip + step, chips)
+        return other, (group, other, column, core)
+
+    barrier = pltpu.get_barrier_semaphore()
+    for step in range(1, chips):
+        pl.semaphore_signal(barrier, inc=1, device_id=peer(step)[1], device_id_type=pl.DeviceIdType.MESH)
+    pl.semaphore_signal(barrier, inc=1, device_id=mate, device_id_type=pl.DeviceIdType.MESH)
+    pl.semaphore_wait(barrier, chips)
+
+    def remote(src, dst, send_sem, recv_sem, device):
+        return pltpu.make_async_remote_copy(
+            src_ref=src,
+            dst_ref=dst,
+            send_sem=send_sem,
+            recv_sem=recv_sem,
+            device_id=device,
+            device_id_type=pl.DeviceIdType.MESH,
+        )
+
+    def near_rows(place):
+        return pl.ds(core * half + place * blocks, blocks)
+
+    def q_rows(place):
+        return pl.ds(place * blocks, blocks)
+
+    def landing(item, h, place):
+        if item == 2:
+            return q_bufs[h].at[q_rows(place)]
+        return (k_bufs, v_bufs)[item][h].at[near_rows(place)]
+
+    sources = (k_ref, v_ref, q_ref)
+
+    def piece(item, h, step):
+        other, device = peer(step)
+        return remote(
+            sources[item].at[other * heads + h],
+            landing(item, h, chip),
+            send.at[h, item, step],
+            recv.at[h, item, step],
+            device,
+        )
+
+    def arriving(item, h, step):
+        sender = lax.rem(chip + chips - step, chips)
+        return remote(
+            sources[item].at[h],
+            landing(item, h, sender),
+            send.at[h, item, step],
+            recv.at[h, item, step],
+            peer(step)[1],
+        )
+
+    def own_piece(item, h):
+        return pltpu.make_async_copy(
+            sources[item].at[chip * heads + h], landing(item, h, chip), own.at[h, item]
+        )
+
+    def list_piece(step):
+        other, device = peer(step)
+        return remote(
+            lists_ref.at[other], lists_in.at[chip], list_send.at[step], list_recv.at[step], device
+        )
+
+    def list_arriving(step):
+        sender = lax.rem(chip + chips - step, chips)
+        return remote(
+            lists_ref.at[0], lists_in.at[sender], list_send.at[step], list_recv.at[step], peer(step)[1]
+        )
+
+    list_own_copy = pltpu.make_async_copy(lists_ref.at[chip], lists_in.at[chip], list_own.at[0])
+    steps = list(range(1, chips))
+    for step in steps:
+        list_piece(step).start()
+    list_own_copy.start()
+    for h in range(heads):
+        for item in range(3):
+            own_piece(item, h).start()
+            for step in steps:
+                piece(item, h, step).start()
+    for step in steps:
+        list_arriving(step).wait_recv()
+    list_own_copy.wait()
+    to_scalars = pltpu.make_async_copy(lists_in, lists, list_own.at[1])
+    to_scalars.start()
+    to_scalars.wait()
+
+    def pair_piece(item, h):
+        mine = pl.ds(core * half, half)
+        buf = (k_bufs, v_bufs)[item][h]
+        return remote(
+            buf.at[mine], buf.at[mine], pair_send.at[h, item], pair_recv.at[h, item], mate
+        )
+
+    def pair_arriving(item, h):
+        other = pl.ds((1 - core) * half, half)
+        buf = (k_bufs, v_bufs)[item][h]
+        return remote(
+            buf.at[other], buf.at[other], pair_send.at[h, item], pair_recv.at[h, item], mate
+        )
+
+    def out_piece(h, step):
+        other, device = peer(step)
+        return remote(
+            o_bufs[h].at[q_rows(other)],
+            out_ref.at[chip * heads + h],
+            out_send.at[h, step],
+            out_recv.at[h, step],
+            device,
+        )
+
+    def out_arriving(h, step):
+        sender = lax.rem(chip + chips - step, chips)
+        return remote(
+            o_bufs[h].at[q_rows(sender)],
+            out_ref.at[sender * heads + h],
+            out_send.at[h, step],
+            out_recv.at[h, step],
+            peer(step)[1],
+        )
+
+    def out_own_piece(h):
+        return pltpu.make_async_copy(
+            o_bufs[h].at[q_rows(chip)], out_ref.at[chip * heads + h], out_own.at[h]
+        )
+
+    exponent_scale = math.log2(math.e) / math.sqrt(width)
+    for h in range(heads):
+        for item in range(2):
+            own_piece(item, h).wait()
+            for step in steps:
+                arriving(item, h, step).wait_recv()
+            pair_piece(item, h).start()
+        own_piece(2, h).wait()
+        for step in steps:
+            arriving(2, h, step).wait_recv()
+        for item in range(2):
+            pair_arriving(item, h).wait_recv()
+
+        k_buf, v_buf, q_buf, o_buf = k_bufs[h], v_bufs[h], q_bufs[h], o_bufs[h]
+        state_sum[...] = jnp.zeros_like(state_sum)
+        total_sum[...] = jnp.zeros_like(total_sum)
+
+        def one_state(j, carry):
+            narrow = wide_feature(k_buf[j]).astype(jnp.bfloat16)
+            state = lax.dot_general(
+                narrow, v_buf[j], (((0,), (0,)), ((), ())), preferred_element_type=jnp.float32
+            )
+            total = jnp.sum(narrow.astype(jnp.float32).reshape(BLOCK // 8, 8, width), axis=0)
+            states[j] = state
+            totals[j] = total
+            state_sum[...] += state
+            total_sum[...] += total
+            return carry
+
+        lax.fori_loop(0, 2 * chips * blocks, one_state, 0, unroll=4)
+
+        def one_block(b, carry):
+            place = b // blocks
+            base = lax.rem(b, blocks) * listed
+            picks = [lists[place, h, base + i] for i in range(listed)]
+            query = q_buf[b]
+            near_keys = jnp.concatenate([k_buf[pick] for pick in picks], axis=0)
+            near_values = jnp.concatenate([v_buf[pick] for pick in picks], axis=0)
+            scores = lax.dot_general(
+                query, near_keys, (((1,), (1,)), ((), ())), preferred_element_type=jnp.float32
+            )
+            top = jnp.max(scores, axis=-1, keepdims=True)
+            expo = jnp.exp2((scores - top) * exponent_scale)
+            mass = jnp.sum(expo, axis=-1, keepdims=True)
+            sparse = jnp.dot(
+                expo.astype(jnp.bfloat16), near_values, preferred_element_type=jnp.float32
+            )
+            state = states[picks[0]]
+            total = totals[picks[0]]
+            for pick in picks[1:]:
+                state = state + states[pick]
+                total = total + totals[pick]
+            state = state_sum[...] - state
+            total = jnp.sum(total_sum[...] - total, axis=0, keepdims=True)
+            coarse = state.astype(jnp.bfloat16)
+            fine = (state - coarse.astype(jnp.float32)).astype(jnp.bfloat16)
+            narrow = wide_feature(query).astype(jnp.bfloat16)
+            numerator = jnp.dot(narrow, coarse, preferred_element_type=jnp.float32) + jnp.dot(
+                narrow, fine, preferred_element_type=jnp.float32
+            )
+            denominator = jnp.sum(narrow.astype(jnp.float32) * total, axis=-1, keepdims=True)
+            linear = (numerator / denominator).astype(jnp.bfloat16)
+            projected = jnp.dot(linear, weight_ref[...], preferred_element_type=jnp.float32)
+            o_buf[b] = (sparse / mass + projected).astype(jnp.bfloat16)
+            return carry
+
+        lax.fori_loop(0, chips * blocks, one_block, 0, unroll=2)
+        for step in steps:
+            out_piece(h, step).start()
+        out_own_piece(h).start()
+
+    for h in range(heads):
+        for item in range(3):
+            for step in steps:
+                piece(item, h, step).wait_send()
+        for item in range(2):
+            pair_piece(item, h).wait_send()
+        out_own_piece(h).wait()
+        for step in steps:
+            out_piece(h, step).wait_send()
+            out_arriving(h, step).wait_recv()
+    for step in steps:
+        list_piece(step).wait_send()
+
+
+def head_major(array):
+    rows, heads, width = array.shape
+    return array.transpose(1, 0, 2).reshape(heads, rows // BLOCK, BLOCK, width)
+
+
+def by_heads(queries, key_rows, value_rows, critical, branch_weight):
+    rows, all_heads, width = queries.shape
+    listed = critical.shape[-1]
+    blocks = rows // BLOCK
+    chips = lax.axis_size("ctx")
+    heads = all_heads // chips
+    shard = critical // blocks
+    place = (shard % 2) * (chips * blocks) + (shard // 2) * blocks + critical % blocks
+    lists = place.transpose(1, 0, 2).reshape(chips, heads, blocks * listed)
+    lists = jnp.pad(lists, ((0, 0), (0, -heads % 8), (0, -(blocks * listed) % 128)))
+    dims = (chips, heads, rows, width, listed)
+    hbm = pl.BlockSpec(memory_space=pl.ANY)
+    vmem = pl.BlockSpec(memory_space=pltpu.VMEM)
+    near = pltpu.VMEM((2 * chips * blocks, BLOCK, width), jnp.bfloat16)
+    mine = pltpu.VMEM((chips * blocks, BLOCK, width), jnp.bfloat16)
+    sem = pltpu.SemaphoreType.DMA
+    all_blocks = 2 * chips * blocks
+    pairs = heads * chips * blocks
+    out = pl.pallas_call(
+        functools.partial(by_heads_kernel, dims),
+        out_shape=jax.ShapeDtypeStruct((all_heads, blocks, BLOCK, width), jnp.bfloat16),
+        in_specs=[hbm, hbm, hbm, hbm, vmem],
+        out_specs=hbm,
+        scratch_shapes=[mine] * heads
+        + [near] * heads
+        + [near] * heads
+        + [mine] * heads
+        + [
+            pltpu.VMEM(lists.shape, jnp.int32),
+            pltpu.SMEM(lists.shape, jnp.int32),
+            pltpu.VMEM((all_blocks, width, width), jnp.float32),
+            pltpu.VMEM((all_blocks, 8, width), jnp.float32),
+            pltpu.VMEM((width, width), jnp.float32),
+            pltpu.VMEM((8, width), jnp.float32),
+            sem((heads, 3, chips)),
+            sem((heads, 3, chips)),
+            sem((heads, 3)),
+            sem((heads, 2)),
+            sem((heads, 2)),
+            sem((heads, chips)),
+            sem((heads, chips)),
+            sem((heads,)),
+            sem((chips,)),
+            sem((chips,)),
+            sem((2,)),
+        ],
+        compiler_params=pltpu.CompilerParams(
+            collective_id=0, has_side_effects=True, vmem_limit_bytes=56 * 1024 * 1024
+        ),
+        cost_estimate=pl.CostEstimate(
+            flops=pairs * 4 * BLOCK * BLOCK * listed * width,
+            bytes_accessed=8 * all_heads * rows * width,
+            transcendentals=pairs * BLOCK * BLOCK * listed,
+        ),
+    )(
+        head_major(queries),
+        head_major(key_rows),
+        head_major(value_rows),
+        lists,
+        branch_weight,
+    )
+    return out.reshape(all_heads, rows, width).transpose(1, 0, 2)
+
+
+def heads_fit(mesh, queries, critical):
+    chips, cores = mesh.shape["ctx"], mesh.shape["sub"]
+    shards = mesh.shape["groups"] * chips * cores
+    rows = queries.shape[0] // shards
+    heads = queries.shape[1] // mesh.shape["head"]
+    if cores != 2 or heads % chips or chips < 2 or rows % BLOCK:
+        return False
+    width = queries.shape[2]
+    tokens = chips * cores * rows
+    held = heads // chips * tokens * width * 2 * 3
+    states = tokens // BLOCK * (width + 8) * width * 4
+    return held + states < 40 * 1024 * 1024
+
+
 def solution(mesh):
     in_specs = (
         P(("groups", "ctx", "sub"), "head", None),
@@ -168,6 +494,12 @@
         P(),
     )
     out_specs = P(("groups", "ctx", "sub"), "head", None)
-    return jax.shard_map(
-        on_device, mesh=mesh, in_specs=in_specs, out_specs=out_specs, check_vma=False
-    )
+
+    def run(queries, key_rows, value_rows, critical, branch_weight):
+        body = by_heads if heads_fit(mesh, queries, critical) else on_device
+        mapped = jax.shard_map(
+            body, mesh=mesh, in_specs=in_specs, out_specs=out_specs, check_vma=False
+        )
+        return mapped(queries, key_rows, value_rows, critical, branch_weight)
+
+    return run

time: 730 us -> 128 us (0.18)
  blocking collectives: 368 us -> 0 us
  local copies, waits for them, and re-layouts: 172 us -> 3.3 us
  Pallas kernels: 0 us -> 124 us
  matrix products: 91.4 us -> 0 us
  other arithmetic: 68.2 us -> 0.82 us
  between operations: 13.5 us -> 0.01 us
  starting transfers between devices: 11.5 us -> 0 us
    psum x1 -> x0, blocking collectives: 197 us -> none  [on_device(): kv_state, key_total = lax.psum((kv_state, key_total), ('ctx', 'sub'))]
    all_to_all x1 -> x0, blocking collectives: 171 us -> none  [on_device(): lax.all_to_all(as_sent((jnp.take(local_keys, picked, axis=0), jnp.take(lo...]
    gather x22 -> x0, local copies, waits for them, and re-layouts: 141 us -> none  [the longest x10 57.2 us: attend_pair(): jnp.take(pool_values, pool_index.reshape(-1), axis=0)]
    pallas_call x0 -> x1, Pallas kernels: none -> 124 us  [by_heads(): pl.pallas_call(functools.partial(by_heads_kernel, dims), out_shape=jax.Sh...]
    dot_general x71 -> x0, matrix products: 91.4 us -> none  [the longest x10 26.9 us: attend_pair(): jnp.einsum('bhqk,bhkd->bhqd', softmax_weights, nearby_value_rows, preferr...]
    select_n x25 -> x0, other arithmetic: 35.6 us -> none  [the longest x20 26.7 us: attend_pair(): jnp.take(pool_keys, pool_index.reshape(-1), axis=0)]
    concatenate x2 -> x0, other arithmetic: 14.7 us -> none  [the longest x1 7.4 us: on_device(): jnp.concatenate([local_keys, far_keys.reshape(shard_count * capacity, 64,...]
    while x20 -> x0, local copies, waits for them, and re-layouts: 13.4 us -> none
  transfers between devices with their start and end apart: 3 -> 0, of which waited for: 1 -> 0; matrix products, arithmetic and copies ran while one was open for 4% -> 0% of each run, Pallas kernels for 0% -> 0%
where the time goes in v1:
time: 128 us
  Pallas kernels  124 us (97%)
  local copies, waits for them, and re-layouts  3.3 us (3%)
    pallas_call x1, Pallas kernels, by_heads(): pl.pallas_call(functools.partial(by_heads_kernel, dims), out_shape=jax.Sh...  124 us

profile of v1, /device:TPU:0, one launch (start us, length us, event | category | flops | bytes accessed | tf_op | source)
XLA Modules:
  0.0 127.7 jit_solution(10047953984433356816)
XLA Ops:
  0.0 0.8 fusion.3
  0.8 0.1 copy.7
  0.9 0.1 reshape.18
  1.0 0.6 pad.4.refs_3_
  1.6 123.6 %shard_map.55 = bf16[20,4,64,128]{3,2,1,0:T(8,128)(2,1)} custom-call(bf16[20,4,64,128]{3,2,1,0:T(8,128)(2,1)} %bitcast.15, bf16[20,4,64,128]{3,2,1,0:T(8,128)(2,1)} %bitcast.16, bf16[20,4,64,128]{3,2,1,0:T(8,128)(2,1)} %bitcast.17, s32[4,8,128]{2,1,0:T(8,128)} %pad.4.refs_3_, bf16[128,128]{1,0:T(8,128)(2,1)} %refs_4_.1), custom_call_target="tpu_custom_call" | custom-call | flops 2684354560 | bytes 5242880 | tf_op jit(solution)/shard_map/pallas_call | solution.py:428
  125.2 2.5 %copy.9 = bf16[256,20,128]{2,0,1:T(8,128)(2,1)} copy(bf16[256,20,128]{2,0,1:T(8,128)(2,1)} %bitcast.14) | data formatting | bytes 2621440

commit v2 on v1

--- a/solution.py
+++ b/solution.py
@@ -173,16 +173,16 @@
 
 
 def by_heads_kernel(dims, *refs):
-    chips, heads, rows, width, listed = dims
+    chips, heads, rows, width = dims
     q_ref, k_ref, v_ref, lists_ref, weight_ref, out_ref = refs[:6]
     refs = refs[6:]
     q_bufs, refs = refs[:heads], refs[heads:]
     k_bufs, refs = refs[:heads], refs[heads:]
     v_bufs, refs = refs[:heads], refs[heads:]
     o_bufs, refs = refs[:heads], refs[heads:]
-    (lists_in, lists, states, totals, state_sum, total_sum) = refs[:6]
-    (send, recv, own, pair_send, pair_recv, out_send, out_recv, out_own) = refs[6:14]
-    list_send, list_recv, list_own = refs[14:]
+    lists_in, members, features = refs[:3]
+    (send, recv, own, pair_send, pair_recv, out_send, out_recv, out_own) = refs[3:11]
+    list_send, list_recv, list_own = refs[11:]
     group = lax.axis_index("groups")
     chip = lax.axis_index("ctx")
     column = lax.axis_index("head")
@@ -274,9 +274,18 @@
     for step in steps:
         list_arriving(step).wait_recv()
     list_own_copy.wait()
-    to_scalars = pltpu.make_async_copy(lists_in, lists, list_own.at[1])
-    to_scalars.start()
-    to_scalars.wait()
+    tokens = 2 * chips * rows
+    lanes = lists_in.shape[-1]
+    spread = (
+        lax.broadcasted_iota(jnp.int32, (lanes, tokens), 1) // BLOCK
+        == lax.broadcasted_iota(jnp.int32, (lanes, tokens), 0)
+    ).astype(jnp.bfloat16)
+    spread_lists = jnp.dot(
+        lists_in[...].reshape(-1, lanes).astype(jnp.bfloat16),
+        spread,
+        preferred_element_type=jnp.float32,
+    )
+    members[...] = spread_lists.reshape(members.shape)
 
     def pair_piece(item, h):
         mine = pl.ds(core * half, half)
@@ -331,59 +340,45 @@
             pair_arriving(item, h).wait_recv()
 
         k_buf, v_buf, q_buf, o_buf = k_bufs[h], v_bufs[h], q_bufs[h], o_bufs[h]
-        state_sum[...] = jnp.zeros_like(state_sum)
-        total_sum[...] = jnp.zeros_like(total_sum)
-
-        def one_state(j, carry):
-            narrow = wide_feature(k_buf[j]).astype(jnp.bfloat16)
-            state = lax.dot_general(
-                narrow, v_buf[j], (((0,), (0,)), ((), ())), preferred_element_type=jnp.float32
+        for j in range(2 * chips):
+            span = pl.ds(j * blocks, blocks)
+            features[span] = wide_feature(k_buf[span]).astype(jnp.bfloat16)
+
+        def one_shard(place, carry):
+            span = pl.ds(place * blocks, blocks)
+            query = q_buf[span].reshape(rows, width)
+            narrow = wide_feature(query).astype(jnp.bfloat16)
+            keys = k_buf[...].reshape(-1, width)
+            key_features = features[...].reshape(-1, width)
+            values = v_buf[...].reshape(-1, width)
+            summed = jnp.concatenate([values, jnp.ones_like(values)], axis=1)
+            scores = lax.dot_general(
+                query, keys, (((1,), (1,)), ((), ())), preferred_element_type=jnp.float32
             )
-            total = jnp.sum(narrow.astype(jnp.float32).reshape(BLOCK // 8, 8, width), axis=0)
-            states[j] = state
-            totals[j] = total
-            state_sum[...] += state
-            total_sum[...] += total
+            far = lax.dot_general(
+                narrow, key_features, (((1,), (1,)), ((), ())), preferred_element_type=jnp.float32
+            )
+            expo, rest = [], []
+            for b in range(blocks):
+                listed_here = members[place, h, b : b + 1, :]
+                part = scores[b * BLOCK : (b + 1) * BLOCK] + (listed_here - 1.0) * 1e30
+                top = jnp.max(part, axis=-1, keepdims=True)
+                expo.append(jnp.exp2((part - top) * exponent_scale).astype(jnp.bfloat16))
+                part = far[b * BLOCK : (b + 1) * BLOCK] * (1.0 - listed_here)
+                rest.append(part.astype(jnp.bfloat16))
+            near_sums = jnp.dot(
+                jnp.concatenate(expo, axis=0), summed, preferred_element_type=jnp.float32
+            )
+            far_sums = jnp.dot(
+                jnp.concatenate(rest, axis=0), summed, preferred_element_type=jnp.float32
+            )
+            linear = (far_sums[:, :width] / far_sums[:, width:]).astype(jnp.bfloat16)
+            projected = jnp.dot(linear, weight_ref[...], preferred_element_type=jnp.float32)
+            mixed = near_sums[:, :width] / near_sums[:, width:] + projected
+            o_buf[span] = mixed.astype(jnp.bfloat16).reshape(blocks, BLOCK, width)
             return carry
 
-        lax.fori_loop(0, 2 * chips * blocks, one_state, 0, unroll=4)
-
-        def one_block(b, carry):
-            place = b // blocks
-            base = lax.rem(b, blocks) * listed
-            picks = [lists[place, h, base + i] for i in range(listed)]
-            query = q_buf[b]
-            near_keys = jnp.concatenate([k_buf[pick] for pick in picks], axis=0)
-            near_values = jnp.concatenate([v_buf[pick] for pick in picks], axis=0)
-            scores = lax.dot_general(
-                query, near_keys, (((1,), (1,)), ((), ())), preferred_element_type=jnp.float32
-            )
-            top = jnp.max(scores, axis=-1, keepdims=True)
-            expo = jnp.exp2((scores - top) * exponent_scale)
-            mass = jnp.sum(expo, axis=-1, keepdims=True)
-            sparse = jnp.dot(
-                expo.astype(jnp.bfloat16), near_values, preferred_element_type=jnp.float32
-            )
-            state = states[picks[0]]
-            total = totals[picks[0]]
-            for pick in picks[1:]:
-                state = state + states[pick]
-                total = total + totals[pick]
-            state = state_sum[...] - state
-            total = jnp.sum(total_sum[...] - total, axis=0, keepdims=True)
-            coarse = state.astype(jnp.bfloat16)
-            fine = (state - coarse.astype(jnp.float32)).astype(jnp.bfloat16)
-            narrow = wide_feature(query).astype(jnp.bfloat16)
-            numerator = jnp.dot(narrow, coarse, preferred_element_type=jnp.float32) + jnp.dot(
-                narrow, fine, preferred_element_type=jnp.float32
-            )
-            denominator = jnp.sum(narrow.astype(jnp.float32) * total, axis=-1, keepdims=True)
-            linear = (numerator / denominator).astype(jnp.bfloat16)
-            projected = jnp.dot(linear, weight_ref[...], preferred_element_type=jnp.float32)
-            o_buf[b] = (sparse / mass + projected).astype(jnp.bfloat16)
-            return carry
-
-        lax.fori_loop(0, chips * blocks, one_block, 0, unroll=2)
+        lax.fori_loop(0, chips, one_shard, 0)
         for step in steps:
             out_piece(h, step).start()
         out_own_piece(h).start()
@@ -409,21 +404,22 @@
 
 def by_heads(queries, key_rows, value_rows, critical, branch_weight):
     rows, all_heads, width = queries.shape
-    listed = critical.shape[-1]
     blocks = rows // BLOCK
     chips = lax.axis_size("ctx")
     heads = all_heads // chips
     shard = critical // blocks
     place = (shard % 2) * (chips * blocks) + (shard // 2) * blocks + critical % blocks
-    lists = place.transpose(1, 0, 2).reshape(chips, heads, blocks * listed)
-    lists = jnp.pad(lists, ((0, 0), (0, -heads % 8), (0, -(blocks * listed) % 128)))
-    dims = (chips, heads, rows, width, listed)
+    all_blocks = 2 * chips * blocks
+    lanes = jnp.arange(all_blocks + -all_blocks % 128, dtype=jnp.int32)
+    lists = jnp.any(place[..., None] == lanes, axis=2).astype(jnp.float32).transpose(1, 0, 2)
+    lists = jnp.pad(lists, ((0, 0), (0, -blocks % 8), (0, 0)))
+    lists = lists.reshape(chips, heads, blocks + -blocks % 8, lanes.shape[0])
+    dims = (chips, heads, rows, width)
     hbm = pl.BlockSpec(memory_space=pl.ANY)
     vmem = pl.BlockSpec(memory_space=pltpu.VMEM)
     near = pltpu.VMEM((2 * chips * blocks, BLOCK, width), jnp.bfloat16)
     mine = pltpu.VMEM((chips * blocks, BLOCK, width), jnp.bfloat16)
     sem = pltpu.SemaphoreType.DMA
-    all_blocks = 2 * chips * blocks
     pairs = heads * chips * blocks
     out = pl.pallas_call(
         functools.partial(by_heads_kernel, dims),
@@ -435,12 +431,9 @@
         + [near] * heads
         + [mine] * heads
         + [
-            pltpu.VMEM(lists.shape, jnp.int32),
-            pltpu.SMEM(lists.shape, jnp.int32),
-            pltpu.VMEM((all_blocks, width, width), jnp.float32),
-            pltpu.VMEM((all_blocks, 8, width), jnp.float32),
-            pltpu.VMEM((width, width), jnp.float32),
-            pltpu.VMEM((8, width), jnp.float32),
+            pltpu.VMEM(lists.shape, jnp.float32),
+            pltpu.VMEM(lists.shape[:3] + (2 * chips * rows,), jnp.float32),
+            near,
             sem((heads, 3, chips)),
             sem((heads, 3, chips)),
             sem((heads, 3)),
@@ -451,15 +444,15 @@
             sem((heads,)),
             sem((chips,)),
             sem((chips,)),
-            sem((2,)),
+            sem((1,)),
         ],
         compiler_params=pltpu.CompilerParams(
             collective_id=0, has_side_effects=True, vmem_limit_bytes=56 * 1024 * 1024
         ),
         cost_estimate=pl.CostEstimate(
-            flops=pairs * 4 * BLOCK * BLOCK * listed * width,
+            flops=pairs * 8 * BLOCK * BLOCK * all_blocks * width,
             bytes_accessed=8 * all_heads * rows * width,
-            transcendentals=pairs * BLOCK * BLOCK * listed,
+            transcendentals=pairs * BLOCK * BLOCK * all_blocks,
         ),
     )(
         head_major(queries),
@@ -481,8 +474,9 @@
     width = queries.shape[2]
     tokens = chips * cores * rows
     held = heads // chips * tokens * width * 2 * 3
-    states = tokens // BLOCK * (width + 8) * width * 4
-    return held + states < 40 * 1024 * 1024
+    members = heads // chips * tokens * 4 * 8 * chips
+    scores = rows * tokens * 4 * 4
+    return held + members + scores < 32 * 1024 * 1024
 
 
 def solution(mesh):

time: 128 us -> 127 us (level)
  Pallas kernels: 124 us -> 122 us
    pallas_call x1, Pallas kernels: 124 us -> 122 us  [by_heads(): pl.pallas_call(functools.partial(by_heads_kernel, dims), out_shape=jax.Sh...]
where the time goes in v2:
time: 127 us
  Pallas kernels  122 us (96%)
  local copies, waits for them, and re-layouts  2.61 us (2%)
  other arithmetic  1.75 us (1%)
    pallas_call x1, Pallas kernels, by_heads(): pl.pallas_call(functools.partial(by_heads_kernel, dims), out_shape=jax.Sh...  122 us

profile of v2, /device:TPU:0, one launch (start us, length us, event | category | flops | bytes accessed | tf_op | source)
XLA Modules:
  0.0 126.7 jit_solution(12330556928103873940)
XLA Ops:
  0.0 0.8 fusion.3
  0.8 0.1 copy.9
  0.9 0.3 fusion
  1.2 0.6 pad_convert_fusion
  1.9 122.3 %shard_map.55 = bf16[20,4,64,128]{3,2,1,0:T(8,128)(2,1)} custom-call(bf16[20,4,64,128]{3,2,1,0:T(8,128)(2,1)} %bitcast.19, bf16[20,4,64,128]{3,2,1,0:T(8,128)(2,1)} %bitcast.20, bf16[20,4,64,128]{3,2,1,0:T(8,128)(2,1)} %bitcast.21, f32[4,5,8,128]{3,2,1,0:T(8,128)} %bitcast.17, bf16[128,128]{1,0:T(8,128)(2,1)} %refs_4_.1), custom_call_target="tpu_custom_call" | custom-call | flops 10737418240 | bytes 5242880 | tf_op jit(solution)/shard_map/pallas_call | solution.py:424
  124.2 2.5 %copy.14 = bf16[256,20,128]{2,0,1:T(8,128)(2,1)} copy(bf16[256,20,128]{2,0,1:T(8,128)(2,1)} %bitcast.16) | data formatting | bytes 2621440
  (1 shorter events, 0.0 us)

commit v3 on v2

--- a/solution.py
+++ b/solution.py
@@ -180,7 +180,10 @@
     k_bufs, refs = refs[:heads], refs[heads:]
     v_bufs, refs = refs[:heads], refs[heads:]
     o_bufs, refs = refs[:heads], refs[heads:]
-    lists_in, members, features = refs[:3]
+    lists_in, members, features, relay, out_relay = refs[:5]
+    relay_send, relay_recv, pass_send, pass_recv = refs[5:9]
+    out_relay_send, out_relay_recv, out_pass_send, out_pass_recv = refs[9:13]
+    refs = refs[10:]
     (send, recv, own, pair_send, pair_recv, out_send, out_recv, out_own) = refs[3:11]
     list_send, list_recv, list_own = refs[11:]
     group = lax.axis_index("groups")
@@ -189,6 +192,8 @@
     core = lax.axis_index("sub")
     blocks = rows // BLOCK
     half = chips * blocks
+    piece_blocks = blocks // 2
+    across = lax.rem(chip + 2, chips)
     mate = (group, chip, column, 1 - core)
 
     def peer(step):
@@ -261,16 +266,101 @@
             lists_ref.at[0], lists_in.at[sender], list_send.at[step], list_recv.at[step], peer(step)[1]
         )
 
+    ways = (1, chips - 1)
+
+    def behind(way):
+        return lax.rem(chip + chips - ways[way], chips)
+
+    def part(way):
+        return pl.ds(way * piece_blocks, piece_blocks)
+
+    def landing_part(item, h, place, way):
+        if item == 2:
+            return q_bufs[h].at[pl.ds(place * blocks + way * piece_blocks, piece_blocks)]
+        first = core * half + place * blocks + way * piece_blocks
+        return (k_bufs, v_bufs)[item][h].at[pl.ds(first, piece_blocks)]
+
+    def relay_piece(item, h, way):
+        return remote(
+            sources[item].at[across * heads + h, part(way)],
+            relay.at[(h * 3 + item) * 2 + way],
+            relay_send.at[h, item, way],
+            relay_recv.at[h, item, way],
+            peer(ways[way])[1],
+        )
+
+    def pass_piece(item, h, way):
+        return remote(
+            relay.at[(h * 3 + item) * 2 + way],
+            landing_part(item, h, behind(way), way),
+            pass_send.at[h, item, way],
+            pass_recv.at[h, item, way],
+            peer(ways[way])[1],
+        )
+
+    def pass_arriving(item, h, way):
+        return remote(
+            relay.at[(h * 3 + item) * 2 + way],
+            landing_part(item, h, across, way),
+            pass_send.at[h, item, way],
+            pass_recv.at[h, item, way],
+            peer(ways[way])[1],
+        )
+
+    def out_relay_piece(h, way):
+        return remote(
+            o_bufs[h].at[pl.ds(across * blocks + way * piece_blocks, piece_blocks)],
+            out_relay.at[h * 2 + way],
+            out_relay_send.at[h, way],
+            out_relay_recv.at[h, way],
+            peer(ways[way])[1],
+        )
+
+    def out_pass_piece(h, way):
+        return remote(
+            out_relay.at[h * 2 + way],
+            out_ref.at[behind(way) * heads + h, part(way)],
+            out_pass_send.at[h, way],
+            out_pass_recv.at[h, way],
+            peer(ways[way])[1],
+        )
+
+    def out_pass_arriving(h, way):
+        return remote(
+            out_relay.at[h * 2 + way],
+            out_ref.at[across * heads + h, part(way)],
+            out_pass_send.at[h, way],
+            out_pass_recv.at[h, way],
+            peer(ways[way])[1],
+        )
+
+    def send_head(h):
+        for item in range(3):
+            for way in range(2):
+                relay_piece(item, h, way).start()
+        for item in range(3):
+            own_piece(item, h).start()
+            for step in ways:
+                piece(item, h, step).start()
+
+    def pass_head(h):
+        for item in range(3):
+            for way in range(2):
+                relay_piece(item, h, way).wait_recv()
+                pass_piece(item, h, way).start()
+
+    def pass_out(h):
+        for way in range(2):
+            out_relay_piece(h, way).wait_recv()
+            out_pass_piece(h, way).start()
+
     list_own_copy = pltpu.make_async_copy(lists_ref.at[chip], lists_in.at[chip], list_own.at[0])
     steps = list(range(1, chips))
     for step in steps:
         list_piece(step).start()
     list_own_copy.start()
-    for h in range(heads):
-        for item in range(3):
-            own_piece(item, h).start()
-            for step in steps:
-                piece(item, h, step).start()
+    for h in range(min(2, heads)):
+        send_head(h)
     for step in steps:
         list_arriving(step).wait_recv()
     list_own_copy.wait()
@@ -328,14 +418,22 @@
 
     exponent_scale = math.log2(math.e) / math.sqrt(width)
     for h in range(heads):
+        if h + 2 < heads:
+            send_head(h + 2)
+        if h == 0:
+            pass_head(0)
+        if h + 1 < heads:
+            pass_head(h + 1)
         for item in range(2):
             own_piece(item, h).wait()
-            for step in steps:
-                arriving(item, h, step).wait_recv()
+            for way in range(2):
+                arriving(item, h, ways[way]).wait_recv()
+                pass_arriving(item, h, way).wait_recv()
             pair_piece(item, h).start()
         own_piece(2, h).wait()
-        for step in steps:
-            arriving(2, h, step).wait_recv()
+        for way in range(2):
+            arriving(2, h, ways[way]).wait_recv()
+            pass_arriving(2, h, way).wait_recv()
         for item in range(2):
             pair_arriving(item, h).wait_recv()
 
@@ -379,20 +477,29 @@
             return carry
 
         lax.fori_loop(0, chips, one_shard, 0)
-        for step in steps:
+        for way in range(2):
+            out_relay_piece(h, way).start()
+        for step in ways:
             out_piece(h, step).start()
         out_own_piece(h).start()
+        if h:
+            pass_out(h - 1)
+    pass_out(heads - 1)
 
     for h in range(heads):
-        for item in range(3):
-            for step in steps:
-                piece(item, h, step).wait_send()
+        for way in range(2):
+            for item in range(3):
+                piece(item, h, ways[way]).wait_send()
+                relay_piece(item, h, way).wait_send()
+                pass_piece(item, h, way).wait_send()
+            out_piece(h, ways[way]).wait_send()
+            out_arriving(h, ways[way]).wait_recv()
+            out_relay_piece(h, way).wait_send()
+            out_pass_piece(h, way).wait_send()
+            out_pass_arriving(h, way).wait_recv()
         for item in range(2):
             pair_piece(item, h).wait_send()
         out_own_piece(h).wait()
-        for step in steps:
-            out_piece(h, step).wait_send()
-            out_arriving(h, step).wait_recv()
     for step in steps:
         list_piece(step).wait_send()
 
@@ -434,6 +541,16 @@
             pltpu.VMEM(lists.shape, jnp.float32),
             pltpu.VMEM(lists.shape[:3] + (2 * chips * rows,), jnp.float32),
             near,
+            pltpu.VMEM((heads * 6, blocks // 2, BLOCK, width), jnp.bfloat16),
+            pltpu.VMEM((heads * 2, blocks // 2, BLOCK, width), jnp.bfloat16),
+            sem((heads, 3, 2)),
+            sem((heads, 3, 2)),
+            sem((heads, 3, 2)),
+            sem((heads, 3, 2)),
+            sem((heads, 2)),
+            sem((heads, 2)),
+            sem((heads, 2)),
+            sem((heads, 2)),
             sem((heads, 3, chips)),
             sem((heads, 3, chips)),
             sem((heads, 3)),
@@ -469,7 +586,7 @@
     shards = mesh.shape["groups"] * chips * cores
     rows = queries.shape[0] // shards
     heads = queries.shape[1] // mesh.shape["head"]
-    if cores != 2 or heads % chips or chips < 2 or rows % BLOCK:
+    if cores != 2 or heads % chips or chips != 4 or rows % (2 * BLOCK):
         return False
     width = queries.shape[2]
     tokens = chips * cores * rows

time: 127 us -> 138 us (1.087)
  Pallas kernels: 122 us -> 133 us
    pallas_call x1, Pallas kernels: 122 us -> 133 us  [by_heads(): pl.pallas_call(functools.partial(by_heads_kernel, dims), out_shape=jax.Sh...]
where the time goes in v3:
time: 138 us; the launch traced here: 137 us
  Pallas kernels  133 us (96%)
  local copies, waits for them, and re-layouts  2.61 us (2%)
  other arithmetic  1.75 us (1%)
    pallas_call x1, Pallas kernels, by_heads(): pl.pallas_call(functools.partial(by_heads_kernel, dims), out_shape=jax.Sh...  133 us

profile of v3, /device:TPU:0, one launch (start us, length us, event | category | flops | bytes accessed | tf_op | source)
XLA Modules:
  0.0 137.5 jit_solution(9270404034983270397)
XLA Ops:
  0.0 0.8 fusion.3
  0.8 0.1 copy.9
  0.9 0.3 fusion
  1.2 0.6 pad_convert_fusion
  1.9 133.1 %shard_map.55 = bf16[20,4,64,128]{3,2,1,0:T(8,128)(2,1)} custom-call(bf16[20,4,64,128]{3,2,1,0:T(8,128)(2,1)} %bitcast.19, bf16[20,4,64,128]{3,2,1,0:T(8,128)(2,1)} %bitcast.20, bf16[20,4,64,128]{3,2,1,0:T(8,128)(2,1)} %bitcast.21, f32[4,5,8,128]{3,2,1,0:T(8,128)} %bitcast.17, bf16[128,128]{1,0:T(8,128)(2,1)} %refs_4_.1), custom_call_target="tpu_custom_call" | custom-call | flops 10737418240 | bytes 5242880 | tf_op jit(solution)/shard_map/pallas_call | solution.py:531
  135.0 2.5 %copy.14 = bf16[256,20,128]{2,0,1:T(8,128)(2,1)} copy(bf16[256,20,128]{2,0,1:T(8,128)(2,1)} %bitcast.16) | data formatting | bytes 2621440
  (1 shorter events, 0.0 us)

commit v4 on v1

--- a/solution.py
+++ b/solution.py
@@ -180,9 +180,9 @@
     k_bufs, refs = refs[:heads], refs[heads:]
     v_bufs, refs = refs[:heads], refs[heads:]
     o_bufs, refs = refs[:heads], refs[heads:]
-    (lists_in, lists, states, totals, state_sum, total_sum) = refs[:6]
-    (send, recv, own, pair_send, pair_recv, out_send, out_recv, out_own) = refs[6:14]
-    list_send, list_recv, list_own = refs[14:]
+    (lists_in, lists, states, totals, scores, sparses, linears) = refs[:7]
+    (send, recv, own, pair_send, pair_recv, out_send, out_recv, out_own) = refs[7:15]
+    list_send, list_recv, list_own = refs[15:]
     group = lax.axis_index("groups")
     chip = lax.axis_index("ctx")
     column = lax.axis_index("head")
@@ -318,12 +318,16 @@
         )
 
     exponent_scale = math.log2(math.e) / math.sqrt(width)
-    for h in range(heads):
+
+    def swap(h):
         for item in range(2):
             own_piece(item, h).wait()
             for step in steps:
                 arriving(item, h, step).wait_recv()
             pair_piece(item, h).start()
+
+    swap(0)
+    for h in range(heads):
         own_piece(2, h).wait()
         for step in steps:
             arriving(2, h, step).wait_recv()
@@ -331,59 +335,69 @@
             pair_arriving(item, h).wait_recv()
 
         k_buf, v_buf, q_buf, o_buf = k_bufs[h], v_bufs[h], q_bufs[h], o_bufs[h]
-        state_sum[...] = jnp.zeros_like(state_sum)
-        total_sum[...] = jnp.zeros_like(total_sum)
+
+        def picks(b, first, count):
+            place = b // blocks
+            base = first * blocks + lax.rem(b, blocks) * count
+            return [lists[place, h, base + i] for i in range(count)]
 
         def one_state(j, carry):
             narrow = wide_feature(k_buf[j]).astype(jnp.bfloat16)
-            state = lax.dot_general(
+            states[j] = lax.dot_general(
                 narrow, v_buf[j], (((0,), (0,)), ((), ())), preferred_element_type=jnp.float32
             )
-            total = jnp.sum(narrow.astype(jnp.float32).reshape(BLOCK // 8, 8, width), axis=0)
-            states[j] = state
-            totals[j] = total
-            state_sum[...] += state
-            total_sum[...] += total
+            totals[j] = jnp.sum(narrow.astype(jnp.float32).reshape(BLOCK // 8, 8, width), axis=0)
             return carry
 
-        lax.fori_loop(0, 2 * chips * blocks, one_state, 0, unroll=4)
-
-        def one_block(b, carry):
-            place = b // blocks
-            base = lax.rem(b, blocks) * listed
-            picks = [lists[place, h, base + i] for i in range(listed)]
-            query = q_buf[b]
-            near_keys = jnp.concatenate([k_buf[pick] for pick in picks], axis=0)
-            near_values = jnp.concatenate([v_buf[pick] for pick in picks], axis=0)
-            scores = lax.dot_general(
-                query, near_keys, (((1,), (1,)), ((), ())), preferred_element_type=jnp.float32
+        def one_score(b, carry):
+            near_keys = jnp.concatenate([k_buf[pick] for pick in picks(b, 0, listed)], axis=0)
+            scores[b] = lax.dot_general(
+                q_buf[b], near_keys, (((1,), (1,)), ((), ())), preferred_element_type=jnp.float32
             )
-            top = jnp.max(scores, axis=-1, keepdims=True)
-            expo = jnp.exp2((scores - top) * exponent_scale)
+            return carry
+
+        def one_linear(b, carry):
+            chosen = picks(b, listed, 2 * chips * blocks - listed)
+            state = states[chosen[0]]
+            total = totals[chosen[0]]
+            for pick in chosen[1:]:
+                state = state + states[pick]
+                total = total + totals[pick]
+            total = jnp.sum(total, axis=0, keepdims=True)
+            coarse = state.astype(jnp.bfloat16)
+            fine = (state - coarse.astype(jnp.float32)).astype(jnp.bfloat16)
+            narrow = wide_feature(q_buf[b]).astype(jnp.bfloat16)
+            numerator = jnp.dot(
+                jnp.concatenate([narrow, narrow], axis=1),
+                jnp.concatenate([coarse, fine], axis=0),
+                preferred_element_type=jnp.float32,
+            )
+            denominator = jnp.sum(narrow.astype(jnp.float32) * total, axis=-1, keepdims=True)
+            linears[b] = (numerator / denominator).astype(jnp.bfloat16)
+            return carry
+
+        def one_sparse(b, carry):
+            near_values = jnp.concatenate([v_buf[pick] for pick in picks(b, 0, listed)], axis=0)
+            here = scores[b]
+            top = jnp.max(here, axis=-1, keepdims=True)
+            expo = jnp.exp2((here - top) * exponent_scale)
             mass = jnp.sum(expo, axis=-1, keepdims=True)
             sparse = jnp.dot(
                 expo.astype(jnp.bfloat16), near_values, preferred_element_type=jnp.float32
             )
-            state = states[picks[0]]
-            total = totals[picks[0]]
-            for pick in picks[1:]:
-                state = state + states[pick]
-                total = total + totals[pick]
-            state = state_sum[...] - state
-            total = jnp.sum(total_sum[...] - total, axis=0, keepdims=True)
-            coarse = state.astype(jnp.bfloat16)
-            fine = (state - coarse.astype(jnp.float32)).astype(jnp.bfloat16)
-            narrow = wide_feature(query).astype(jnp.bfloat16)
-            numerator = jnp.dot(narrow, coarse, preferred_element_type=jnp.float32) + jnp.dot(
-                narrow, fine, preferred_element_type=jnp.float32
-            )
-            denominator = jnp.sum(narrow.astype(jnp.float32) * total, axis=-1, keepdims=True)
-            linear = (numerator / denominator).astype(jnp.bfloat16)
-            projected = jnp.dot(linear, weight_ref[...], preferred_element_type=jnp.float32)
-            o_buf[b] = (sparse / mass + projected).astype(jnp.bfloat16)
+            sparses[b] = sparse / mass
             return carry
 
-        lax.fori_loop(0, chips * blocks, one_block, 0, unroll=2)
+        lax.fori_loop(0, chips * blocks, one_score, 0, unroll=4)
+        lax.fori_loop(0, 2 * chips * blocks, one_state, 0, unroll=8)
+        if h + 1 < heads:
+            swap(h + 1)
+        lax.fori_loop(0, chips * blocks, one_sparse, 0, unroll=4)
+        lax.fori_loop(0, chips * blocks, one_linear, 0, unroll=4)
+        projected = jnp.dot(
+            linears[...].reshape(-1, width), weight_ref[...], preferred_element_type=jnp.float32
+        )
+        o_buf[...] = (sparses[...] + projected.reshape(sparses.shape)).astype(jnp.bfloat16)
         for step in steps:
             out_piece(h, step).start()
         out_own_piece(h).start()
@@ -415,15 +429,27 @@
     heads = all_heads // chips
     shard = critical // blocks
     place = (shard % 2) * (chips * blocks) + (shard // 2) * blocks + critical % blocks
-    lists = place.transpose(1, 0, 2).reshape(chips, heads, blocks * listed)
-    lists = jnp.pad(lists, ((0, 0), (0, -heads % 8), (0, -(blocks * listed) % 128)))
+    all_blocks = 2 * chips * blocks
+    every = jnp.arange(all_blocks, dtype=jnp.int32)
+    unlisted = jnp.all(place[..., None] != every, axis=2)
+    earlier = jnp.logical_and(unlisted[..., None, :], every[None, :] < every[:, None])
+    rank = jnp.where(unlisted, jnp.sum(earlier.astype(jnp.int32), axis=-1), -1)
+    ranks = jnp.arange(all_blocks - listed, dtype=jnp.int32)
+    others = jnp.sum(jnp.where(rank[..., None, :] == ranks[:, None], every, 0), axis=-1)
+    lists = jnp.concatenate(
+        [
+            rows_of.transpose(1, 0, 2).reshape(chips, heads, -1)
+            for rows_of in (place, others)
+        ],
+        axis=-1,
+    )
+    lists = jnp.pad(lists, ((0, 0), (0, -heads % 8), (0, -lists.shape[-1] % 128)))
     dims = (chips, heads, rows, width, listed)
     hbm = pl.BlockSpec(memory_space=pl.ANY)
     vmem = pl.BlockSpec(memory_space=pltpu.VMEM)
     near = pltpu.VMEM((2 * chips * blocks, BLOCK, width), jnp.bfloat16)
     mine = pltpu.VMEM((chips * blocks, BLOCK, width), jnp.bfloat16)
     sem = pltpu.SemaphoreType.DMA
-    all_blocks = 2 * chips * blocks
     pairs = heads * chips * blocks
     out = pl.pallas_call(
         functools.partial(by_heads_kernel, dims),
@@ -439,8 +465,9 @@
             pltpu.SMEM(lists.shape, jnp.int32),
             pltpu.VMEM((all_blocks, width, width), jnp.float32),
             pltpu.VMEM((all_blocks, 8, width), jnp.float32),
-            pltpu.VMEM((width, width), jnp.float32),
-            pltpu.VMEM((8, width), jnp.float32),
+            pltpu.VMEM((chips * blocks, BLOCK, listed * BLOCK), jnp.float32),
+            pltpu.VMEM((chips * blocks, BLOCK, width), jnp.float32),
+            mine,
             sem((heads, 3, chips)),
             sem((heads, 3, chips)),
             sem((heads, 3)),
@@ -482,7 +509,10 @@
     tokens = chips * cores * rows
     held = heads // chips * tokens * width * 2 * 3
     states = tokens // BLOCK * (width + 8) * width * 4
-    return held + states < 40 * 1024 * 1024
+    scores = chips * rows * (critical.shape[2] * BLOCK + 2 * width) * 4
+    if critical.shape[2] >= tokens // BLOCK:
+        return False
+    return held + states + scores < 40 * 1024 * 1024
 
 
 def solution(mesh):

time: 128 us -> 130 us (1.016)
  other arithmetic: 0.82 us -> 4.89 us
  Pallas kernels: 124 us -> 121 us
    reduce_sum x0 -> x2, other arithmetic: none -> 2.85 us  [the longest x1 1.43 us: by_heads(): rank = jnp.where(unlisted, jnp.sum(earlier.astype(jnp.int32), axis=-1), -1)]
    pallas_call x1, Pallas kernels: 124 us -> 121 us  [by_heads(): pl.pallas_call(functools.partial(by_heads_kernel, dims), out_shape=jax.Sh...]
where the time goes in v4:
time: 130 us; the launch traced here: 129 us
  Pallas kernels  121 us (93%)
  other arithmetic  4.89 us (4%)
  local copies, waits for them, and re-layouts  3.5 us (3%)
    pallas_call x1, Pallas kernels, by_heads(): pl.pallas_call(functools.partial(by_heads_kernel, dims), out_shape=jax.Sh...  121 us

profile of v4, /device:TPU:0, one launch (start us, length us, event | category | flops | bytes accessed | tf_op | source)
XLA Modules:
  0.0 129.2 jit_solution(12540760632684327577)
XLA Ops:
  0.0 0.8 fusion.11
  0.8 0.1 copy.10
  0.9 0.1 reshape.40
  1.0 0.8 fusion.3
  1.9 0.1 copy.11
  2.0 0.3 fusion
  2.2 1.4 %convert_reduce_fusion = s32[4,20,32]{2,1,0:T(8,128)S(1)} fusion(pred[32,32]{1,0:T(8,128)(4,1)S(1)} %iota_compare_fusion.2, pred[4,20,32]{2,1,0:T(8,128)(4,1)S(1)} %fusion), kind=kLoop, calls=%fused_computation | loop fusion | flops 243200 | bytes 13824 | tf_op jit(solution)/shard_map/reduce_sum | solution.py:436
  3.7 1.4 %select_reduce_fusion = s32[4,20,16]{2,1,0:T(8,128)S(1)} fusion(s32[4,20,32]{2,1,0:T(8,128)S(1)} %broadcast_select_fusion), kind=kLoop, calls=%fused_computation.1 | loop fusion | flops 121600 | bytes 15360 | tf_op jit(solution)/shard_map/reduce_sum | solution.py:438
  5.1 0.1 reshape.41
  5.2 0.1 pad_add_fusion
  5.3 0.6 pad.4.refs_3_
  5.9 120.8 %shard_map.55 = bf16[20,4,64,128]{3,2,1,0:T(8,128)(2,1)} custom-call(bf16[20,4,64,128]{3,2,1,0:T(8,128)(2,1)} %bitcast.17, bf16[20,4,64,128]{3,2,1,0:T(8,128)(2,1)} %bitcast.18, bf16[20,4,64,128]{3,2,1,0:T(8,128)(2,1)} %bitcast.19, s32[4,8,128]{2,1,0:T(8,128)} %pad.4.refs_3_, bf16[128,128]{1,0:T(8,128)(2,1)} %refs_4_.1), custom_call_target="tpu_custom_call" | custom-call | flops 2684354560 | bytes 5242880 | tf_op jit(solution)/shard_map/pallas_call | solution.py:454
  126.7 2.5 %copy.14 = bf16[256,20,128]{2,0,1:T(8,128)(2,1)} copy(bf16[256,20,128]{2,0,1:T(8,128)(2,1)} %bitcast.15) | data formatting | bytes 2621440
  (3 shorter events, 0.0 us)

commit v5 on v2

--- a/solution.py
+++ b/solution.py
@@ -266,11 +266,18 @@
     for step in steps:
         list_piece(step).start()
     list_own_copy.start()
+
+    def send_rows(item, h):
+        for step in steps:
+            piece(item, h, step).start()
+        own_piece(item, h).start()
+
     for h in range(heads):
-        for item in range(3):
-            own_piece(item, h).start()
-            for step in steps:
-                piece(item, h, step).start()
+        send_rows(0, h)
+        send_rows(1, h)
+        if h:
+            send_rows(2, h - 1)
+    send_rows(2, heads - 1)
     for step in steps:
         list_arriving(step).wait_recv()
     list_own_copy.wait()
@@ -327,15 +334,18 @@
         )
 
     exponent_scale = math.log2(math.e) / math.sqrt(width)
-    for h in range(heads):
+
+    def swap(h):
         for item in range(2):
             own_piece(item, h).wait()
             for step in steps:
                 arriving(item, h, step).wait_recv()
             pair_piece(item, h).start()
-        own_piece(2, h).wait()
-        for step in steps:
-            arriving(2, h, step).wait_recv()
+
+    swap(0)
+    for h in range(heads):
+        if h + 1 < heads:
+            swap(h + 1)
         for item in range(2):
             pair_arriving(item, h).wait_recv()
 
@@ -344,7 +354,17 @@
             span = pl.ds(j * blocks, blocks)
             features[span] = wide_feature(k_buf[span]).astype(jnp.bfloat16)
 
-        def one_shard(place, carry):
+        def one_shard(step, carry):
+            place = lax.rem(chip + chips - step, chips)
+
+            @pl.when(step == 0)
+            def _():
+                own_piece(2, h).wait()
+
+            @pl.when(step > 0)
+            def _():
+                arriving(2, h, step).wait_recv()
+
             span = pl.ds(place * blocks, blocks)
             query = q_buf[span].reshape(rows, width)
             narrow = wide_feature(query).astype(jnp.bfloat16)
@@ -376,12 +396,18 @@
             projected = jnp.dot(linear, weight_ref[...], preferred_element_type=jnp.float32)
             mixed = near_sums[:, :width] / near_sums[:, width:] + projected
             o_buf[span] = mixed.astype(jnp.bfloat16).reshape(blocks, BLOCK, width)
+
+            @pl.when(step == 0)
+            def _():
+                out_own_piece(h).start()
+
+            @pl.when(step > 0)
+            def _():
+                out_piece(h, chips - step).start()
+
             return carry
 
         lax.fori_loop(0, chips, one_shard, 0)
-        for step in steps:
-            out_piece(h, step).start()
-        out_own_piece(h).start()
 
     for h in range(heads):
         for item in range(3):

time: 127 us -> 128 us (level)
  no operation moved by 1% of the time
where the time goes in v5:
time: 128 us; the launch traced here: 127 us
  Pallas kernels  123 us (96%)
  local copies, waits for them, and re-layouts  2.61 us (2%)
  other arithmetic  1.75 us (1%)
    pallas_call x1, Pallas kernels, by_heads(): pl.pallas_call(functools.partial(by_heads_kernel, dims), out_shape=jax.Sh...  123 us

profile of v5, /device:TPU:0, one launch (start us, length us, event | category | flops | bytes accessed | tf_op | source)
XLA Modules:
  0.0 127.5 jit_solution(1321430919248850869)
XLA Ops:
  0.0 0.8 fusion.3
  0.8 0.1 copy.9
  0.9 0.3 fusion
  1.2 0.6 pad_convert_fusion
  1.9 123.1 %shard_map.55 = bf16[20,4,64,128]{3,2,1,0:T(8,128)(2,1)} custom-call(bf16[20,4,64,128]{3,2,1,0:T(8,128)(2,1)} %bitcast.19, bf16[20,4,64,128]{3,2,1,0:T(8,128)(2,1)} %bitcast.20, bf16[20,4,64,128]{3,2,1,0:T(8,128)(2,1)} %bitcast.21, f32[4,5,8,128]{3,2,1,0:T(8,128)} %bitcast.17, bf16[128,128]{1,0:T(8,128)(2,1)} %refs_4_.1), custom_call_target="tpu_custom_call" | custom-call | flops 10737418240 | bytes 5242880 | tf_op jit(solution)/shard_map/pallas_call | solution.py:450
  125.0 2.5 %copy.14 = bf16[256,20,128]{2,0,1:T(8,128)(2,1)} copy(bf16[256,20,128]{2,0,1:T(8,128)(2,1)} %bitcast.16) | data formatting | bytes 2621440
  (1 shorter events, 0.0 us)

commit v6 on v5

--- a/solution.py
+++ b/solution.py
@@ -272,12 +272,10 @@
             piece(item, h, step).start()
         own_piece(item, h).start()
 
-    for h in range(heads):
+    for h in range(min(2, heads)):
         send_rows(0, h)
         send_rows(1, h)
-        if h:
-            send_rows(2, h - 1)
-    send_rows(2, heads - 1)
+    send_rows(2, 0)
     for step in steps:
         list_arriving(step).wait_recv()
     list_own_copy.wait()
@@ -344,7 +342,11 @@
 
     swap(0)
     for h in range(heads):
+        if h + 2 < heads:
+            send_rows(0, h + 2)
+            send_rows(1, h + 2)
         if h + 1 < heads:
+            send_rows(2, h + 1)
             swap(h + 1)
         for item in range(2):
             pair_arriving(item, h).wait_recv()

time: 128 us -> 131 us (1.023)
  Pallas kernels: 123 us -> 126 us
    pallas_call x1, Pallas kernels: 123 us -> 126 us  [by_heads(): pl.pallas_call(functools.partial(by_heads_kernel, dims), out_shape=jax.Sh...]
where the time goes in v6:
time: 131 us; the launch traced here: 130 us
  Pallas kernels  126 us (96%)
  local copies, waits for them, and re-layouts  2.61 us (2%)
  other arithmetic  1.75 us (1%)
    pallas_call x1, Pallas kernels, by_heads(): pl.pallas_call(functools.partial(by_heads_kernel, dims), out_shape=jax.Sh...  126 us

profile of v6, /device:TPU:0, one launch (start us, length us, event | category | flops | bytes accessed | tf_op | source)
XLA Modules:
  0.0 130.5 jit_solution(3432787992352936413)
XLA Ops:
  0.0 0.8 fusion.3
  0.8 0.1 copy.9
  0.9 0.3 fusion
  1.2 0.6 pad_convert_fusion
  1.9 126.1 %shard_map.55 = bf16[20,4,64,128]{3,2,1,0:T(8,128)(2,1)} custom-call(bf16[20,4,64,128]{3,2,1,0:T(8,128)(2,1)} %bitcast.19, bf16[20,4,64,128]{3,2,1,0:T(8,128)(2,1)} %bitcast.20, bf16[20,4,64,128]{3,2,1,0:T(8,128)(2,1)} %bitcast.21, f32[4,5,8,128]{3,2,1,0:T(8,128)} %bitcast.17, bf16[128,128]{1,0:T(8,128)(2,1)} %refs_4_.1), custom_call_target="tpu_custom_call" | custom-call | flops 10737418240 | bytes 5242880 | tf_op jit(solution)/shard_map/pallas_call | solution.py:452
  128.0 2.5 %copy.14 = bf16[256,20,128]{2,0,1:T(8,128)(2,1)} copy(bf16[256,20,128]{2,0,1:T(8,128)(2,1)} %bitcast.16) | data formatting | bytes 2621440
  (1 shorter events, 0.0 us)
